TPU v7x, 32 devices: a whole 2x2x4 slice. The times are simulated.
32 devices in a mesh: tok: 4 (over y, x), ch: 8 (over z, core).
Axes of the slice: x: 2, y: 2, z: 4, core: 2. Of those that a mesh axis runs over, the one named last changes fastest.
Arguments:
- tokens: bfloat16 [64, 16384], P('tok', 'ch'), may hold values from -64 to 64
- probe: int32 [64, 16384], P('tok', 'ch'), may hold values from 0 to 1
- signs: int32 [16384], P('ch'), may hold values from 0 to 1
- gate_weight: bfloat16 [16384, 26624], P('ch', 'tok'), may hold values from -0.046875 to 0.046875
- up_weight: bfloat16 [16384, 26624], P('ch', 'tok'), may hold values from -0.046875 to 0.046875
- down_weight: bfloat16 [26624, 16384], P('tok', 'ch'), may hold values from -0.0390625 to 0.0390625
Outputs:
- rotated_product: float32 [64, 16384], P('tok', 'ch')
- diagonal_estimate: float32 [16384], P('ch')
All inputs are finite; a program needn't handle non-finite values.
Results may differ from a plain program's by a relative error of at most 0.004.
Values may be sent and summed in bfloat16 or wider, within the bound.
A program may use at most 192 MiB of HBM per device.

v0:
```python
import math

import jax
import jax.numpy as jnp
from jax import lax
from jax.sharding import PartitionSpec as P

D = 16384


def partner_2(value, axis, stride):
    mask = 2**stride
    pairs = [(source, source ^ mask) for source in range(lax.axis_size(axis))]
    return lax.ppermute(value, axis, pairs)


def sign_table(length):
    indices = jnp.arange(length, dtype=jnp.int32)
    parity = jnp.zeros((length, length), jnp.int32)
    for bit_pos in range(length.bit_length() - 1):
        parity = parity + (indices[:, None] >> bit_pos & 1) * (indices[None, :] >> bit_pos & 1)
    return jnp.where(parity % 2 == 0, 1.0, -1.0).astype(jnp.float32)


def cross_pairs(values):
    my_index = lax.axis_index("ch")
    for bit_pos in range(lax.axis_size("ch").bit_length() - 1):
        partner = partner_2(values, "ch", bit_pos)
        upper_half = my_index >> bit_pos & 1 == 1
        values = jnp.where(upper_half, partner - values, values + partner)
    return values


def cross_section(values):
    return cross_pairs(values)


def grad_product(gate_piece, up_piece, gate_weight, up_weight):
    contract = (((1,), (1,)), ((), ()))
    first_term = lax.dot_general(
        gate_piece, gate_weight, contract, preferred_element_type=jnp.float32
    )
    return first_term + lax.dot_general(
        up_piece, up_weight, contract, preferred_element_type=jnp.float32
    )


def on_device(tokens, probe, signs, gate_weight, up_weight, down_weight):
    tok_rows, channels = tokens.shape
    total_rows = tok_rows * lax.axis_size("tok")
    root_scale = 1.0 / math.sqrt(D)
    hadamard = sign_table(channels)
    probe_signs = (2 * probe - 1).astype(jnp.float32)
    channel_signs = (2 * signs - 1).astype(jnp.float32)
    start_local = jnp.dot(
        (probe_signs * channel_signs[None, :]).astype(jnp.bfloat16),
        hadamard.astype(jnp.bfloat16),
        preferred_element_type=jnp.float32,
    )
    tangent = (cross_section(start_local) * root_scale).astype(jnp.bfloat16)
    all_tokens, all_tangent = (
        lax.all_gather(tokens, "tok", axis=0, tiled=True),
        lax.all_gather(tangent, "tok", axis=0, tiled=True),
    )
    inputs = jnp.stack([all_tokens, all_tangent], axis=1)
    gate_part = jnp.einsum("rsd,df->rsf", inputs, gate_weight, preferred_element_type=jnp.float32)
    up_part = jnp.einsum("rsd,df->rsf", inputs, up_weight, preferred_element_type=jnp.float32)
    summed = lax.psum_scatter(
        jnp.stack([gate_part, up_part], axis=2), "ch", scatter_dimension=0, tiled=True
    )
    gate_pre = summed[:, 0, 0]
    up_pre = summed[:, 0, 1]
    gate_tan = summed[:, 1, 0]
    up_tan = summed[:, 1, 1]
    sigmoid_gate = jax.nn.sigmoid(gate_pre)
    activated = gate_pre * sigmoid_gate
    slope_term = sigmoid_gate * (1.0 + gate_pre * (1.0 - sigmoid_gate))
    hidden_tan = (slope_term * gate_tan * up_pre + activated * up_tan).astype(jnp.bfloat16)
    out_part = jnp.dot(
        lax.all_gather(hidden_tan, "ch", axis=0, tiled=True),
        down_weight,
        preferred_element_type=jnp.float32,
    )
    out_tangent = lax.psum(out_part, "tok").astype(jnp.bfloat16)
    piece = out_tangent
    back_hidden = lax.psum_scatter(
        lax.dot_general(
            piece, down_weight, (((1,), (1,)), ((), ())), preferred_element_type=jnp.float32
        ),
        "ch",
        scatter_dimension=0,
        tiled=True,
    )
    back_gate = (back_hidden * up_pre * slope_term).astype(jnp.bfloat16)
    back_up = (back_hidden * activated).astype(jnp.bfloat16)
    stacked = jnp.stack([back_gate, back_up], axis=1)
    piece = lax.all_gather(stacked, "ch", axis=0, tiled=True)
    in_part = grad_product(piece[:, 0], piece[:, 1], gate_weight, up_weight)
    back_tokens = lax.psum_scatter(in_part, "tok", scatter_dimension=0, tiled=True)
    local_back = jnp.dot(
        back_tokens, hadamard, precision=lax.Precision.HIGHEST, preferred_element_type=jnp.float32
    )
    rotated_product = cross_section(local_back) * root_scale * channel_signs[None, :]
    token_terms = jnp.sum(probe_signs * rotated_product, axis=0)
    diagonal_estimate = lax.psum(token_terms, "tok") / total_rows
    return (rotated_product, diagonal_estimate)


def solution(mesh):
    placed = (
        P("tok", "ch"),
        P("tok", "ch"),
        P("ch"),
        P("ch", "tok"),
        P("ch", "tok"),
        P("tok", "ch"),
    )
    return jax.shard_map(
        on_device, mesh=mesh, in_specs=placed, out_specs=(P("tok", "ch"), P("ch")), check_vma=False
    )
```

profile of v0, /device:TPU:0, one launch (start us, length us, event | category | flops | bytes accessed | tf_op | source)
XLA Modules:
  0.0 390.4 jit_solution(12572476447981984975)
XLA Ops:
  8.0 22.7 %fusion.7 = pred[2048,2048]{1,0:T(32,128)(4,1)S(1)} fusion(s32[2048]{0:T(1024)S(1)} %get-tuple-element.6, s32[2048]{0:T(1024)S(1)} %get-tuple-element.7, s32[2048]{0:T(1024)S(1)} %get-tuple-element.8, s32[2048]{0:T(1024)S(1)} %get-tuple-element.9, s32[2048]{0:T(1024)S(1)} %get-tuple-element.10, s32[2048]{0:T(1024)S(1)} %get-tuple-element.11, ...), kind=kLoop, calls=%fused_computation.11 | loop fusion | flops 138412032 | bytes 4284416 | tf_op jit(solution)/shard_map/eq | solution.py:22
  32.8 2.9 fusion.14
  37.2 3.0 collective-permute-start.1
  40.2 3.8 collective-permute-done.1
  44.0 2.8 collective-permute-start.2
  46.8 9.3 %all_gather.12 = bf16[64,2048]{1,0:T(8,128)(2,1)S(1)} all-gather(bf16[16,2048]{1,0:T(8,128)(2,1)} %param.6), channel_id=1, replica_groups=mesh['tok'=4,'ch'=8] {'tok'}, dimensions={0}, use_global_device_ids=true | all-gather | bytes 327680 | tf_op jit(solution)/shard_map/all_gather | solution.py:62
  56.1 8.7 %all_gather.13 = bf16[64,2048]{1,0:T(8,128)(2,1)S(1)} all-gather(bf16[16,2048]{1,0:T(8,128)(2,1)S(1)} %multiply_convert_fusion.2), channel_id=1, replica_groups=mesh['tok'=4,'ch'=8] {'tok'}, dimensions={0}, use_global_device_ids=true | all-gather | bytes 327680 | tf_op jit(solution)/shard_map/all_gather | solution.py:63
  64.8 10.7 %fusion.11 = f32[64,2,1,6656]{3,0,1,2:T(8,128)S(1)} fusion(bf16[2048,6656]{1,0:T(8,128)(2,1)} %param.10, bf16[64,1,2048]{2,0,1:T(8,128)(2,1)S(1)} %bitcast.79, bf16[64,1,2048]{2,0,1:T(8,128)(2,1)S(1)} %bitcast.77), kind=kOutput, calls=%fused_computation.13 | convolution fusion | flops 3489923072 | bytes 31195136 | tf_op jit(solution)/shard_map/rsd,df->rsf/dot_general | solution.py:67
  75.5 10.7 %fusion.8 = f32[64,2,1,6656]{3,0,1,2:T(8,128)S(1)} fusion(bf16[2048,6656]{1,0:T(8,128)(2,1)} %param.9, bf16[64,1,2048]{2,0,1:T(8,128)(2,1)S(1)} %bitcast.80, bf16[64,1,2048]{2,0,1:T(8,128)(2,1)S(1)} %bitcast.78), kind=kOutput, calls=%fused_computation.12 | convolution fusion | flops 3489923072 | bytes 31195136 | tf_op jit(solution)/shard_map/rsd,df->rsf/dot_general | solution.py:66
  86.3 3.4 pad_maximum_fusion
  89.7 73.3 %reduce-scatter.4.cloned.1.call-done = f32[8,2,2,6656]{3,0,1,2:T(8,128)} async-done(((f32[64,2,2,6656]{3,0,1,2:T(8,128)}), f32[8,2,2,6656]{3,0,1,2:T(8,128)}) %reduce-scatter.4.cloned.1.call-update) | async-done | bytes 851984 | tf_op jit(solution)/shard_map/reduce_scatter | solution.py:68
  164.3 16.1 %all_gather.14 = bf16[64,6656]{1,0:T(8,128)(2,1)S(1)} all-gather(bf16[8,6656]{1,0:T(8,128)(2,1)S(1)} %fusion.24), channel_id=1, replica_groups=mesh['tok'=4,'ch'=8] {'ch'}, dimensions={0}, use_global_device_ids=true | all-gather | bytes 958464 | tf_op jit(solution)/shard_map/all_gather | solution.py:80
  180.4 11.2 %fusion.41 = f32[64,2048]{1,0:T(8,128)S(1)} fusion(bf16[64,6656]{1,0:T(8,128)(2,1)S(1)} %all_gather.14, bf16[6656,2048]{1,0:T(8,128)(2,1)} %param.11), kind=kOutput, calls=%fused_computation.78 | convolution fusion | flops 1744830464 | bytes 28639232 | tf_op jit(solution)/shard_map/dot_general | solution.py:79
  191.7 27.6 %all-reduce.1 = bf16[64,2048]{1,0:T(8,128)(2,1)S(1)} all-reduce(f32[64,2048]{1,0:T(8,128)S(1)} %fusion.41), channel_id=1, replica_groups=mesh['tok'=4,'ch'=8] {'tok'}, use_global_device_ids=true, to_apply=%region_1.2 | all-reduce | flops 131072 | bytes 786432 | tf_op jit(solution)/shard_map/psum | solution.py:84
  219.3 14.7 %fusion.42 = f32[64,6656]{1,0:T(8,128)} fusion(bf16[64,2048]{1,0:T(8,128)(2,1)S(1)} %all-reduce.1, bf16[6656,2048]{1,0:T(8,128)(2,1)} %param.11), kind=kOutput, calls=%fused_computation.79 | convolution fusion | flops 1744830464 | bytes 29229056 | tf_op jit(solution)/shard_map/dot_general | solution.py:87
  234.1 32.0 %reduce-scatter.6.cloned.1.call-done = f32[8,6656]{1,0:T(8,128)} async-done(((f32[64,6656]{1,0:T(8,128)}), f32[8,6656]{1,0:T(8,128)}) %reduce-scatter.6.cloned.1.call-update) | async-done | bytes 213008 | tf_op jit(solution)/shard_map/reduce_scatter | solution.py:86
  268.1 23.5 %all-gather.2.cloned.1.call-done = bf16[64,2,6656]{2,0,1:T(8,128)(2,1)} async-done(((bf16[8,2,6656]{2,0,1:T(8,128)(2,1)}), bf16[64,2,6656]{2,0,1:T(8,128)(2,1)}) %all-gather.2.cloned.1.call-update) | async-done | bytes 1703952 | tf_op jit(solution)/shard_map/all_gather | solution.py:97
  291.6 17.1 %fusion.19 = f32[64,2048]{1,0:T(8,128)S(1)} fusion(bf16[2048,6656]{1,0:T(8,128)(2,1)} %param.9, bf16[64,2,6656]{2,0,1:T(8,128)(2,1)} %all-gather.2.cloned.1.call-done), kind=kOutput, calls=%fused_computation.23 | convolution fusion | flops 1744830464 | bytes 28639232 | tf_op jit(solution)/shard_map/dot_general | solution.py:40
  308.8 14.2 %convolution_add_fusion = f32[64,2048]{1,0:T(8,128)} fusion(f32[64,2048]{1,0:T(8,128)S(1)} %fusion.19, bf16[2048,6656]{1,0:T(8,128)(2,1)} %param.10, bf16[64,2,6656]{2,0,1:T(8,128)(2,1)S(1)} %copy-done), kind=kOutput, calls=%fused_computation.20 | convolution fusion | flops 1744961536 | bytes 29163520 | tf_op jit(solution)/shard_map/dot_general | solution.py:43
  323.0 24.5 %reduce-scatter.8.cloned.1.call-done = f32[16,2048]{1,0:T(8,128)} async-done(((f32[64,2048]{1,0:T(8,128)}), f32[16,2048]{1,0:T(8,128)}) %reduce-scatter.8.cloned.1.call-update) | async-done | bytes 131088 | tf_op jit(solution)/shard_map/reduce_scatter | solution.py:99
  347.4 10.5 %fusion.4 = f32[16,2048]{1,0:T(8,128)S(1)} fusion(f32[16,2048]{1,0:T(8,128)} %reduce-scatter.8.cloned.1.call-done, pred[2048,2048]{1,0:T(32,128)(4,1)} %copy-done.1), kind=kOutput, calls=%fused_computation.7 | convolution fusion | flops 809500672 | bytes 4456448 | tf_op jit(solution)/shard_map/dot_general | solution.py:100
  360.9 4.1 %collective-permute-done.4 = f32[16,2048]{1,0:T(8,128)S(1)} collective-permute-done((f32[16,2048]{1,0:T(8,128)S(1)}, f32[16,2048]{1,0:T(8,128)S(1)}, u32[]{:S(2)}, u32[]{:S(2)}) %collective-permute-start.4) | collective-permute-done | bytes 131104 | tf_op jit(solution)/shard_map/ppermute | solution.py:14
  367.5 6.0 %collective-permute-done.5 = f32[16,2048]{1,0:T(8,128)S(1)} collective-permute-done((f32[16,2048]{1,0:T(8,128)S(1)}, f32[16,2048]{1,0:T(8,128)S(1)}, u32[]{:S(2)}, u32[]{:S(2)}) %collective-permute-start.5) | collective-permute-done | bytes 131104 | tf_op jit(solution)/shard_map/ppermute | solution.py:14
  374.2 9.0 %psum.15 = f32[2048]{0:T(1024)S(1)} all-reduce(f32[2048]{0:T(1024)S(1)} %get-tuple-element.2), channel_id=1, replica_groups=mesh['tok'=4,'ch'=8] {'tok'}, use_global_device_ids=true, to_apply=%region_5.6 | all-reduce | flops 2048 | bytes 16384 | tf_op jit(solution)/shard_map/psum | solution.py:105
  (43 shorter events, 14.6 us)
Async XLA Ops:
  7.2 155.8 %reduce-scatter.4.cloned.1.call-start = ((), (), s32[]{:S(2)}) async-start(), calls=%async_computation.3 | async-start | bytes 7667712 | tf_op jit(solution)/shard_map/reduce_scatter | solution.py:68
  30.7 2.1 copy-start.1
  35.7 1.4 collective-permute-start
  37.2 6.8 %collective-permute-start.1 = (f32[16,2048]{1,0:T(8,128)S(1)}, f32[16,2048]{1,0:T(8,128)S(1)}, u32[]{:S(2)}, u32[]{:S(2)}) collective-permute-start(f32[16,2048]{1,0:T(8,128)S(1)} %add_select_fusion.4), channel_id=1, source_target_pairs={{0,2},{1,3},{2,0},{3,1},{4,6},{5,7},{6,4},{7,5},{8,10},{9,11},{10,... | collective-permute-start | bytes 393224 | tf_op jit(solution)/shard_map/ppermute | solution.py:14
  44.0 12.1 %collective-permute-start.2 = (f32[16,2048]{1,0:T(8,128)S(1)}, f32[16,2048]{1,0:T(8,128)S(1)}, u32[]{:S(2)}, u32[]{:S(2)}) collective-permute-start(f32[16,2048]{1,0:T(8,128)S(1)} %add_select_fusion.3), channel_id=1, source_target_pairs={{0,4},{1,5},{2,6},{3,7},{4,0},{5,1},{6,2},{7,3},{8,12},{9,13},{10,... | collective-permute-start | bytes 393224 | tf_op jit(solution)/shard_map/ppermute | solution.py:14
  89.7 176.4 %reduce-scatter.6.cloned.1.call-start = ((), (), s32[]{:S(2)}) async-start(), calls=%async_computation.4 | async-start | bytes 1916928 | tf_op jit(solution)/shard_map/reduce_scatter | solution.py:86
  219.3 46.7 %copy-start.2 = (f32[8,2,2,6656]{3,0,1,2:T(8,128)S(1)}, f32[8,2,2,6656]{3,0,1,2:T(8,128)}, u32[]{:S(2)}) copy-start(f32[8,2,2,6656]{3,0,1,2:T(8,128)} %reduce-scatter.4.cloned.1.call-done) | copy-start | bytes 2555908
  234.0 57.6 %all-gather.2.cloned.1.call-start = ((), (), s32[]{:S(2)}) async-start(), calls=%async_computation.5 | async-start | bytes 1916928 | tf_op jit(solution)/shard_map/all_gather | solution.py:97
  267.8 79.6 %reduce-scatter.8.cloned.1.call-start = ((), (), s32[]{:S(2)}) async-start(), calls=%async_computation.6 | async-start | bytes 655360 | tf_op jit(solution)/shard_map/reduce_scatter | solution.py:99
  291.6 17.2 %copy-start = (bf16[64,2,6656]{2,0,1:T(8,128)(2,1)S(1)}, bf16[64,2,6656]{2,0,1:T(8,128)(2,1)}, u32[]{:S(2)}) copy-start(bf16[64,2,6656]{2,0,1:T(8,128)(2,1)} %all-gather.2.cloned.1.call-done) | copy-start | bytes 5111812
  308.8 58.7 %copy-start.4 = (s32[2048]{0:T(1024)S(1)}, s32[2048]{0:T(1024)}, u32[]{:S(2)}) copy-start(s32[2048]{0:T(1024)} %param.8) | copy-start | bytes 24580
  308.8 64.7 %copy-start.3 = (s32[16,2048]{1,0:T(8,128)S(1)}, s32[16,2048]{1,0:T(8,128)}, u32[]{:S(2)}) copy-start(s32[16,2048]{1,0:T(8,128)} %param.7) | copy-start | bytes 393220
  358.0 1.4 collective-permute-start.3
  359.4 5.6 %collective-permute-start.4 = (f32[16,2048]{1,0:T(8,128)S(1)}, f32[16,2048]{1,0:T(8,128)S(1)}, u32[]{:S(2)}, u32[]{:S(2)}) collective-permute-start(f32[16,2048]{1,0:T(8,128)S(1)} %add_select_fusion.2), channel_id=1, source_target_pairs={{0,2},{1,3},{2,0},{3,1},{4,6},{5,7},{6,4},{7,5},{8,10},{9,11},{10,... | collective-permute-start | bytes 393224 | tf_op jit(solution)/shard_map/ppermute | solution.py:14
  365.0 8.5 %collective-permute-start.5 = (f32[16,2048]{1,0:T(8,128)S(1)}, f32[16,2048]{1,0:T(8,128)S(1)}, u32[]{:S(2)}, u32[]{:S(2)}) collective-permute-start(f32[16,2048]{1,0:T(8,128)S(1)} %add_select_fusion.1), channel_id=1, source_target_pairs={{0,4},{1,5},{2,6},{3,7},{4,0},{5,1},{6,2},{7,3},{8,12},{9,13},{10,... | collective-permute-start | bytes 393224 | tf_op jit(solution)/shard_map/ppermute | solution.py:14
Sparse Core Ops, SparseCore 0:
  89.8 73.1 reduce-scatter.3
  234.1 31.8 reduce-scatter.5
  267.9 23.6 all-gather.1
  323.1 24.3 reduce-scatter.7
where the time goes:
time: 391 us; the launch traced here: 390 us
  waiting for transfers between devices  169 us (43%)
  matrix products  92.1 us (24%)
  blocking collectives  70.7 us (18%)
  other arithmetic  31.3 us (8%)
  between operations  13.9 us (4%)
  starting transfers between devices  10.7 us (3%)
    reduce_scatter x1, waiting for transfers between devices, on_device(): lax.psum_scatter(jnp.stack([gate_part, up_part], axis=2), 'ch', scatter_d...  73.3 us
    reduce_scatter x1, waiting for transfers between devices, on_device(): lax.psum_scatter(lax.dot_general(piece, down_weight, (((1,), (1,)), ((),...  32 us
    psum x1, blocking collectives, on_device(): out_tangent = lax.psum(out_part, 'tok').astype(jnp.bfloat16)  27.6 us
    reduce_scatter x1, waiting for transfers between devices, on_device(): lax.psum_scatter(in_part, 'tok', scatter_dimension=0, tiled=True)  24.5 us
    all_gather x1, waiting for transfers between devices, on_device(): piece = lax.all_gather(stacked, 'ch', axis=0, tiled=True)  23.5 us
    eq x1, other arithmetic, sign_table(): return jnp.where(parity % 2 == 0, 1.0, -1.0).astype(jnp.float32)  22.7 us
    dot_general x1, matrix products, grad_product(): lax.dot_general(gate_piece, gate_weight, contract, preferred_element_type...  17.1 us
    ppermute x6, waiting for transfers between devices, partner_2(): return lax.ppermute(value, axis, pairs)  16.2 us
  transfers between devices with their start and end apart: 10, of which 9 were waited for; matrix products, arithmetic and copies ran while one was open for 0% of the time, Pallas kernels for 0%

commit v1 on v0

v1 whole, which is shorter than its diff:
```python
import functools
import math

import jax
import jax.numpy as jnp
from jax import lax
from jax.experimental import pallas as pl
from jax.experimental.pallas import tpu as pltpu
from jax.sharding import PartitionSpec as P

D = 16384
VMEM_LIMIT = 63 * 1024 * 1024


def partner_2(value, axis, stride):
    mask = 2**stride
    pairs = [(source, source ^ mask) for source in range(lax.axis_size(axis))]
    return lax.ppermute(value, axis, pairs)


def local_rotation(values):
    rows, length = values.shape
    lane = 128
    index = jnp.arange(lane, dtype=jnp.int32)
    parity = lax.population_count(index[:, None] & index[None, :]) & 1
    inner = jnp.where(parity == 0, 1.0, -1.0).astype(jnp.float32)
    values = jnp.dot(
        values.reshape(rows * (length // lane), lane),
        inner,
        precision=lax.Precision.HIGHEST,
        preferred_element_type=jnp.float32,
    ).reshape(rows, length // lane, lane)
    span = 1
    while span < length // lane:
        pairs = values.reshape(rows, length // lane // (2 * span), 2, span, lane)
        low, high = pairs[:, :, 0], pairs[:, :, 1]
        values = jnp.stack([low + high, low - high], axis=2)
        span *= 2
    return values.reshape(rows, length)


def cross_pairs(values):
    my_index = lax.axis_index("ch")
    for bit_pos in range(lax.axis_size("ch").bit_length() - 1):
        partner = partner_2(values, "ch", bit_pos)
        upper_half = my_index >> bit_pos & 1 == 1
        values = jnp.where(upper_half, partner - values, values + partner)
    return values


def cross_section(values):
    return cross_pairs(values)


SLOTS = 3
NT = (((1,), (1,)), ((), ()))


def layer_kernel(dims, x_in, gate_hbm, up_hbm, down_hbm, out_ref, *scratch):
    shards, rows, zs, chunks, width = dims
    (
        x, gate_buf, up_buf, down_buf, sums, to_sib, from_sib, from_z, slope_up, active, hid,
        out_acc, o_send, o_recv, o_all, sums2, to_sib2, from_sib2, to_z2, from_z2, grads,
        in_acc, k_send, k_recv,
        gate_sem, up_sem, down_sem, x_ss, x_rs, os_ss, os_rs, og_ss, og_rs, k_ss, k_rs,
        a_ss, a_rs, b_ss, b_rs, d_ss, d_rs, s_ss, s_rs,
        a2_ss, a2_rs, b2_ss, b2_rs, d2_ss, d2_rs, s2_ss, s2_rs,
    ) = scratch
    tok = lax.axis_index("tok")
    ch = lax.axis_index("ch")
    z, core = ch // 2, ch % 2
    per = shards // 4
    quarter = per * rows
    last = zs - 1
    f32, bf16 = jnp.float32, jnp.bfloat16

    def loads(f):
        slot = lax.rem(f, SLOTS)
        cols = pl.ds(pl.multiple_of(f * width, width), width)
        return (
            pltpu.make_async_copy(gate_hbm.at[:, cols], gate_buf.at[slot], gate_sem.at[slot]),
            pltpu.make_async_copy(up_hbm.at[:, cols], up_buf.at[slot], up_sem.at[slot]),
        )

    def load_down(f):
        at = pl.ds(pl.multiple_of(f * width, width), width)
        return pltpu.make_async_copy(down_hbm.at[at, :], down_buf.at[f], down_sem.at[f])

    def remote(src, dst, ss, rs, t, c):
        return pltpu.make_async_remote_copy(
            src_ref=src, dst_ref=dst, send_sem=ss, recv_sem=rs,
            device_id=(t, c), device_id_type=pl.DeviceIdType.MESH,
        )

    for f in range(SLOTS):
        for copy in loads(f):
            copy.start()

    sib = z * 2 + 1 - core
    barrier = pltpu.get_barrier_semaphore()

    def greet(t, c):
        pl.semaphore_signal(
            barrier, inc=1, device_id=(t, c), device_id_type=pl.DeviceIdType.MESH
        )

    for d in range(1, shards):
        greet(lax.rem(tok + d, shards), ch)
    greet(tok, sib)
    pl.when(z > 0)(lambda: greet(tok, ch - 2))
    pl.when(z < last)(lambda: greet(tok, ch + 2))
    inner = jnp.logical_and(z > 0, z < last)
    pl.when(inner)(lambda: pl.semaphore_wait(barrier, shards + 2))
    pl.when(jnp.logical_not(inner))(lambda: pl.semaphore_wait(barrier, shards + 1))

    def place(s):
        owner = s // per
        side = lax.rem(owner % 2 + core, 2)
        return (side * 2 + owner // 2) * per + s % per

    def peers(make):
        return [make(d, lax.rem(tok + d, shards)) for d in range(1, shards)]

    mine = pl.ds(pl.multiple_of(place(tok) * 2 * rows, 2 * rows), 2 * rows)
    x[mine, :] = x_in[...]
    gathers = peers(
        lambda d, p: remote(x_in, x.at[mine, :], x_ss.at[d - 1], x_rs.at[d - 1], p, ch)
    )
    for copy in gathers:
        copy.start()
    for copy in gathers:
        copy.wait()

    def ends():
        for e in range(2):
            far = last - z if e == 0 else z
            near = z if e == 0 else last - z
            toward = ch - 2 if e == 0 else ch + 2
            away = ch + 2 if e == 0 else ch - 2
            yield e, far, near, toward, away

    def in_range(f):
        return jnp.logical_and(f >= 0, f < chunks)

    def when(*conditions):
        return pl.when(functools.reduce(jnp.logical_and, conditions))

    def line(i, chunk_at, part, add_sib, a_copy, recv, b_copy, finish, block, d_copy, s_copy):
        n1 = i - 1

        @pl.when(in_range(n1))
        def _():
            a_copy(chunk_at(n1)).wait_recv()
            add_sib(chunk_at(n1))

        for e, far, near, toward, away in ends():
            n2 = i - 1 - far

            @pl.when(in_range(n2))
            def _():
                f = chunk_at(n2)

                @pl.when(far > 0)
                def _():
                    b_copy(e, f, toward).wait_recv()
                    recv(e, f)

                @pl.when(near > 0)
                def _():
                    part(e, f)
                    b_copy(e, f, toward).start()

                @pl.when(near == 0)
                def _():
                    finish(e, f)
                    d_copy(e, f, away).start()
                    s_copy(e, f).start()

            n3 = i - 1 - last - near

            @when(in_range(n3), near > 0)
            def _():
                f = chunk_at(n3)
                d_copy(e, f, away).wait_recv()

                @pl.when(far > 0)
                def _():
                    d_copy(e, f, away).start()

                s_copy(e, f).start()

    def drain(a_copy, b_copy, d_copy, s_copy):
        def body(f, carry):
            a_copy(f).wait_send()
            for e, far, near, toward, away in ends():
                pl.when(near > 0)(lambda: b_copy(e, f, toward).wait_send())
                pl.when(far > 0)(lambda: d_copy(e, f, away).wait_send())
                s_copy(e, f).wait_send()
            return carry

        lax.fori_loop(0, chunks, body, 0)

    lag = 2 + 2 * last

    def block_of(e):
        return pl.ds(pl.multiple_of((e * 2 + core) * quarter, quarter), quarter)

    half = pl.ds(0, 2 * quarter)

    def a_copy(f):
        return remote(to_sib.at[f], from_sib.at[f], a_ss.at[f], a_rs.at[f], tok, sib)

    def b_copy(e, f, c):
        return remote(
            sums.at[f, e], from_z.at[f, e], b_ss.at[e, f], b_rs.at[e, f], tok, c
        )

    def d_copy(e, f, c):
        ref = hid.at[f, block_of(e), :]
        return remote(ref, ref, d_ss.at[e, f], d_rs.at[e, f], tok, c)

    def s_copy(e, f):
        ref = hid.at[f, block_of(e), :]
        return remote(ref, ref, s_ss.at[e, f], s_rs.at[e, f], tok, sib)

    def sib_recv(e, f):
        other = pl.ds(pl.multiple_of((e * 2 + 1 - core) * quarter, quarter), quarter)
        ref = hid.at[f, other, :]
        return remote(ref, ref, s_ss.at[e, f], s_rs.at[e, f], tok, sib)

    def add_sib(f):
        sums[f] += from_sib[f]

    def recv(e, f):
        sums[f, e] += from_z[f, e]

    def finish(e, f):
        for p in range(per):
            base = p * 2 * rows
            gate_pre = sums[f, e, base : base + rows, :width]
            up_pre = sums[f, e, base : base + rows, width:]
            gate_tan = sums[f, e, base + rows : base + 2 * rows, :width]
            up_tan = sums[f, e, base + rows : base + 2 * rows, width:]
            sig = jax.nn.sigmoid(gate_pre)
            act = gate_pre * sig
            slope = sig * (1.0 + gate_pre * (1.0 - sig))
            su = slope * up_pre
            slope_up[f, p * rows : (p + 1) * rows, :] = su
            active[f, p * rows : (p + 1) * rows, :] = act
            at = (e * 2 + core) * quarter + p * rows
            hid[f, pl.ds(pl.multiple_of(at, rows), rows), :] = (
                su * gate_tan + act * up_tan
            ).astype(bf16)

    out_acc[...] = jnp.zeros_like(out_acc)

    def forward(i, carry):
        @pl.when(i < chunks)
        def _():
            load_down(i).start()
            for copy in loads(i):
                copy.wait()
            slot = lax.rem(i, SLOTS)
            for n, buf in enumerate((gate_buf, up_buf)):
                part = jnp.dot(x[...], buf[slot], preferred_element_type=f32)
                cols = slice(n * width, (n + 1) * width)
                for e in range(2):
                    sums[i, e, :, cols] = part[e * 2 * quarter : (e + 1) * 2 * quarter]
                to_sib[i, 0, :, cols] = part[4 * quarter : 6 * quarter]
                to_sib[i, 1, :, cols] = part[6 * quarter :]
            a_copy(i).start()

            @pl.when(i + SLOTS < chunks)
            def _():
                for copy in loads(i + SLOTS):
                    copy.start()

        line(
            i, lambda n: n, lambda e, f: None, add_sib, a_copy, recv, b_copy, finish, None,
            d_copy, s_copy,
        )
        n4 = i - lag

        @pl.when(n4 >= 0)
        def _():
            for e in range(2):
                sib_recv(e, n4).wait_recv()
            load_down(n4).wait()
            out_acc[...] += jnp.dot(hid[n4], down_buf[n4], preferred_element_type=f32)

        return carry

    lax.fori_loop(0, chunks + lag, forward, 0)
    drain(a_copy, b_copy, d_copy, s_copy)

    def scatter(acc, send, recv, ss, rs):
        send[...] = acc[...].astype(bf16)

        def make(d, p):
            at = pl.ds(pl.multiple_of(p * rows, rows), rows)
            return remote(send.at[at, :], recv.at[d - 1], ss.at[d - 1], rs.at[d - 1], p, ch)

        copies = peers(make)
        for copy in copies:
            copy.start()
        total = acc[pl.ds(pl.multiple_of(tok * rows, rows), rows), :]
        for d, copy in enumerate(copies):
            copy.wait()
            total = total + recv[d].astype(f32)
        return total

    here = pl.ds(pl.multiple_of(place(tok) * rows, rows), rows)
    o_all[here, :] = scatter(out_acc, o_send, o_recv, os_ss, os_rs).astype(bf16)
    gathers = peers(
        lambda d, p: remote(
            o_all.at[here, :], o_all.at[here, :], og_ss.at[d - 1], og_rs.at[d - 1], p, ch
        )
    )
    for copy in gathers:
        copy.start()
    for d, copy in enumerate(gathers):
        copy.wait()

    def a2_copy(f):
        return remote(to_sib2.at[f], from_sib2.at[f], a2_ss.at[f], a2_rs.at[f], tok, sib)

    def b2_copy(e, f, c):
        return remote(
            to_z2.at[f, e], from_z2.at[f, e], b2_ss.at[e, f], b2_rs.at[e, f], tok, c
        )

    def d2_copy(e, f, c):
        ref = grads.at[f, e * 2 + core]
        return remote(ref, ref, d2_ss.at[e, f], d2_rs.at[e, f], tok, c)

    def s2_copy(e, f):
        ref = grads.at[f, e * 2 + core]
        return remote(ref, ref, s2_ss.at[e, f], s2_rs.at[e, f], tok, sib)

    def sib2_recv(e, f):
        ref = grads.at[f, e * 2 + 1 - core]
        return remote(ref, ref, s2_ss.at[e, f], s2_rs.at[e, f], tok, sib)

    def add_sib2(f):
        sums2[f] += from_sib2[f]

    def recv2(e, f):
        sums2[f, e] += from_z2[f, e].astype(f32)

    def part2(e, f):
        to_z2[f, e] = sums2[f, e].astype(bf16)

    def finish2(e, f):
        back = sums2[f, e]
        grads[f, e * 2 + core, 0] = (back * slope_up[f]).astype(bf16)
        grads[f, e * 2 + core, 1] = (back * active[f]).astype(bf16)

    def chunk_at(n):
        return chunks - 1 - n

    in_acc[...] = jnp.zeros_like(in_acc)

    def backward(i, carry):
        @pl.when(i < chunks)
        def _():
            f = chunk_at(i)
            part = lax.dot_general(o_all[...], down_buf[f], NT, preferred_element_type=f32)
            for e in range(2):
                sums2[f, e] = part[e * quarter : (e + 1) * quarter]
                to_sib2[f, e] = part[(2 + e) * quarter : (3 + e) * quarter]
            a2_copy(f).start()

        line(
            i, chunk_at, part2, add_sib2, a2_copy, recv2, b2_copy, finish2, None, d2_copy, s2_copy
        )
        n4 = i - lag

        @pl.when(n4 >= 0)
        def _():
            f = chunk_at(n4)
            for e in range(2):
                sib2_recv(e, f).wait_recv()

            @pl.when(f + SLOTS < chunks)
            def _():
                for copy in loads(f):
                    copy.wait()

            slot = lax.rem(f, SLOTS)
            both = grads[f]
            for n, buf in enumerate((gate_buf, up_buf)):
                piece = both[:, n].reshape(4 * quarter, width)
                in_acc[...] += lax.dot_general(piece, buf[slot], NT, preferred_element_type=f32)

            @pl.when(f >= SLOTS)
            def _():
                for copy in loads(f - SLOTS):
                    copy.start()

        return carry

    lax.fori_loop(0, chunks + lag, backward, 0)
    drain(a2_copy, b2_copy, d2_copy, s2_copy)
    out_ref[...] = scatter(in_acc, k_send, k_recv, k_ss, k_rs)


def layer(local, gate_weight, up_weight, down_weight):
    shards, ways = lax.axis_size("tok"), lax.axis_size("ch")
    rows, depth = local.shape[0] // 2, local.shape[1]
    hidden = gate_weight.shape[1]
    width = max(w for w in range(128, 513, 128) if hidden % w == 0)
    chunks = hidden // width
    total, quarter = shards * rows, shards * rows // 4
    dims = (shards, rows, ways // 2, chunks, width)
    f32, bf16, vmem = jnp.float32, jnp.bfloat16, pltpu.VMEM
    dma = pltpu.SemaphoreType.DMA
    scratch = [
        vmem((2 * total, depth), bf16),
        vmem((SLOTS, depth, width), bf16),
        vmem((SLOTS, depth, width), bf16),
        vmem((chunks, width, depth), bf16),
        vmem((chunks, 2, 2 * quarter, 2 * width), f32),
        vmem((chunks, 2, 2 * quarter, 2 * width), f32),
        vmem((chunks, 2, 2 * quarter, 2 * width), f32),
        vmem((chunks, 2, 2 * quarter, 2 * width), f32),
        vmem((chunks, quarter, width), f32),
        vmem((chunks, quarter, width), f32),
        vmem((chunks, total, width), bf16),
        vmem((total, depth), f32),
        vmem((total, depth), bf16),
        vmem((shards - 1, rows, depth), bf16),
        vmem((total, depth), bf16),
        vmem((chunks, 2, quarter, width), f32),
        vmem((chunks, 2, quarter, width), f32),
        vmem((chunks, 2, quarter, width), f32),
        vmem((chunks, 2, quarter, width), bf16),
        vmem((chunks, 2, quarter, width), bf16),
        vmem((chunks, 4, 2, quarter, width), bf16),
        vmem((total, depth), f32),
        vmem((total, depth), bf16),
        vmem((shards - 1, rows, depth), bf16),
        dma((SLOTS,)), dma((SLOTS,)), dma((chunks,)),
        *[dma((shards - 1,)) for _ in range(8)],
    ]
    for _ in range(2):
        scratch += [dma((chunks,)), dma((chunks,))]
        scratch += [dma((2, chunks)) for _ in range(6)]
    flops = 2 * total * depth * hidden * 8
    return pl.pallas_call(
        functools.partial(layer_kernel, dims),
        out_shape=jax.ShapeDtypeStruct((rows, depth), f32),
        in_specs=[pl.BlockSpec(memory_space=vmem)] + [pl.BlockSpec(memory_space=pl.ANY)] * 3,
        out_specs=pl.BlockSpec(memory_space=vmem),
        scratch_shapes=scratch,
        compiler_params=pltpu.CompilerParams(
            collective_id=0, has_side_effects=True, vmem_limit_bytes=VMEM_LIMIT
        ),
        cost_estimate=pl.CostEstimate(
            flops=flops, bytes_accessed=10 * depth * hidden, transcendentals=0
        ),
    )(local, gate_weight, up_weight, down_weight)


def on_device(tokens, probe, signs, gate_weight, up_weight, down_weight):
    tok_rows, channels = tokens.shape
    total_rows = tok_rows * lax.axis_size("tok")
    root_scale = 1.0 / math.sqrt(D)
    probe_signs = (2 * probe - 1).astype(jnp.float32)
    channel_signs = (2 * signs - 1).astype(jnp.float32)
    start_local = local_rotation(probe_signs * channel_signs[None, :])
    tangent = (cross_section(start_local) * root_scale).astype(jnp.bfloat16)
    back_tokens = layer(
        jnp.concatenate([tokens, tangent], axis=0), gate_weight, up_weight, down_weight
    )
    local_back = local_rotation(back_tokens)
    rotated_product = cross_section(local_back) * root_scale * channel_signs[None, :]
    token_terms = jnp.sum(probe_signs * rotated_product, axis=0)
    diagonal_estimate = lax.psum(token_terms, "tok") / total_rows
    return (rotated_product, diagonal_estimate)


def solution(mesh):
    placed = (
        P("tok", "ch"),
        P("tok", "ch"),
        P("ch"),
        P("ch", "tok"),
        P("ch", "tok"),
        P("tok", "ch"),
    )
    return jax.shard_map(
        on_device, mesh=mesh, in_specs=placed, out_specs=(P("tok", "ch"), P("ch")), check_vma=False
    )
```

time: 391 us -> 212 us (0.54)
  Pallas kernels: 0 us -> 162 us
  waiting for transfers between devices: 169 us -> 26 us
  matrix products: 92.1 us -> 0.53 us
  blocking collectives: 70.7 us -> 9.32 us
  other arithmetic: 31.3 us -> 4.76 us
  between operations: 13.9 us -> 0.88 us
  starting transfers between devices: 10.7 us -> 6.59 us
    pallas_call x0 -> x1, Pallas kernels: none -> 162 us  [layer(): pl.pallas_call(functools.partial(layer_kernel, dims), out_shape=jax.Shape...]
    reduce_scatter x3 -> x0, waiting for transfers between devices: 130 us -> none  [the longest x1 73.3 us: on_device(): lax.psum_scatter(jnp.stack([gate_part, up_part], axis=2), 'ch', scatter_d...]
    dot_general x8 -> x2, matrix products: 92.1 us -> 0.53 us  [local_rotation(): jnp.dot(values.reshape(rows * (length // lane), lane), inner, precision=l...]
    all_gather x3 -> x0, blocking collectives: 34 us -> none  [the longest x1 16.1 us: on_device(): lax.all_gather(hidden_tan, 'ch', axis=0, tiled=True)]
    psum x1 -> x0, blocking collectives: 27.6 us -> none  [on_device(): out_tangent = lax.psum(out_part, 'tok').astype(jnp.bfloat16)]
    all_gather x1 -> x0, waiting for transfers between devices: 23.5 us -> none  [on_device(): piece = lax.all_gather(stacked, 'ch', axis=0, tiled=True)]
    eq x1 -> x0, other arithmetic: 22.7 us -> none  [sign_table(): return jnp.where(parity % 2 == 0, 1.0, -1.0).astype(jnp.float32)]
    ppermute x6, waiting for transfers between devices: 16.2 us -> 26 us  [partner_2(): return lax.ppermute(value, axis, pairs)]
  transfers between devices with their start and end apart: 10 -> 6, of which waited for: 9 -> 6; matrix products, arithmetic and copies ran while one was open for 0% -> 0% of each run, Pallas kernels for 0% -> 0%
where the time goes in v1:
time: 212 us; the launch traced here: 211 us
  Pallas kernels  162 us (76%)
  waiting for transfers between devices  26 us (12%)
  blocking collectives  9.32 us (4%)
  starting transfers between devices  6.59 us (3%)
  other arithmetic  4.76 us (2%)
    pallas_call x1, Pallas kernels, layer(): pl.pallas_call(functools.partial(layer_kernel, dims), out_shape=jax.Shape...  162 us
    ppermute x6, waiting for transfers between devices, partner_2(): return lax.ppermute(value, axis, pairs)  26 us
    psum x1, blocking collectives, on_device(): diagonal_estimate = lax.psum(token_terms, 'tok') / total_rows  9.32 us
    ppermute x6, starting transfers between devices, partner_2(): return lax.ppermute(value, axis, pairs)  6.59 us
  transfers between devices with their start and end apart: 6, of which 6 were waited for; matrix products, arithmetic and copies ran while one was open for 0% of the time, Pallas kernels for 0%

profile of v1, /device:TPU:0, one launch (start us, length us, event | category | flops | bytes accessed | tf_op | source)
XLA Modules:
  0.0 211.2 jit_solution(5855541817002783367)
XLA Ops:
  0.6 0.7 add_convert_fusion
  1.3 0.9 convert_multiply_fusion
  2.3 0.1 dot_general.14
  2.4 0.3 convolution_bitcast_fusion.1
  2.9 0.5 collective-permute-start
  3.4 1.0 collective-permute-done
  4.4 3.0 %collective-permute-start.1 = (f32[16,2048]{1,0:T(8,128)S(1)}, f32[16,2048]{1,0:T(8,128)S(1)}, u32[]{:S(2)}, u32[]{:S(2)}) collective-permute-start(f32[16,2048]{1,0:T(8,128)S(1)} %add_select_fusion.3), channel_id=1, source_target_pairs={{0,2},{1,3},{2,0},{3,1},{4,6},{5,7},{6,4},{7,5},{8,10},{9,11},{10,... | collective-permute-start | bytes 393224 | tf_op jit(solution)/shard_map/ppermute | solution.py:18
  7.4 3.8 %collective-permute-done.1 = f32[16,2048]{1,0:T(8,128)S(1)} collective-permute-done((f32[16,2048]{1,0:T(8,128)S(1)}, f32[16,2048]{1,0:T(8,128)S(1)}, u32[]{:S(2)}, u32[]{:S(2)}) %collective-permute-start.1) | collective-permute-done | bytes 131104 | tf_op jit(solution)/shard_map/ppermute | solution.py:18
  11.3 2.8 %collective-permute-start.2 = (f32[16,2048]{1,0:T(8,128)S(1)}, f32[16,2048]{1,0:T(8,128)S(1)}, u32[]{:S(2)}, u32[]{:S(2)}) collective-permute-start(f32[16,2048]{1,0:T(8,128)S(1)} %add_select_fusion.2), channel_id=1, source_target_pairs={{0,4},{1,5},{2,6},{3,7},{4,0},{5,1},{6,2},{7,3},{8,12},{9,13},{10,... | collective-permute-start | bytes 393224 | tf_op jit(solution)/shard_map/ppermute | solution.py:18
  14.1 6.0 %collective-permute-done.2 = f32[16,2048]{1,0:T(8,128)S(1)} collective-permute-done((f32[16,2048]{1,0:T(8,128)S(1)}, f32[16,2048]{1,0:T(8,128)S(1)}, u32[]{:S(2)}, u32[]{:S(2)}) %collective-permute-start.2) | collective-permute-done | bytes 131104 | tf_op jit(solution)/shard_map/ppermute | solution.py:18
  20.1 1.5 pad_maximum_fusion.3.x_in
  21.6 161.8 %shard_map.77 = f32[16,2048]{1,0:T(8,128)} custom-call(bf16[32,2048]{1,0:T(8,128)(2,1)} %pad_maximum_fusion.3.x_in, bf16[2048,6656]{1,0:T(8,128)(2,1)} %gate_hbm.1, bf16[2048,6656]{1,0:T(8,128)(2,1)} %up_hbm.1, bf16[6656,2048]{1,0:T(8,128)(2,1)} %down_hbm.1), custom_call_target="tpu_custom_call" | custom-call | flops 13958643712 | bytes 136314880 | tf_op jit(solution)/shard_map/pallas_call | solution.py:449
  183.5 1.0 dot_general.17
  184.5 0.3 convolution_bitcast_fusion
  185.0 0.1 collective-permute-start.3
  185.1 1.3 collective-permute-done.3
  186.5 0.1 collective-permute-start.4
  186.6 5.5 %collective-permute-done.4 = f32[16,2048]{1,0:T(8,128)S(1)} collective-permute-done((f32[16,2048]{1,0:T(8,128)S(1)}, f32[16,2048]{1,0:T(8,128)S(1)}, u32[]{:S(2)}, u32[]{:S(2)}) %collective-permute-start.4) | collective-permute-done | bytes 131104 | tf_op jit(solution)/shard_map/ppermute | solution.py:18
  192.1 0.1 collective-permute-start.5
  192.2 0.0 copy-done.1
  192.2 8.4 %collective-permute-done.5 = f32[16,2048]{1,0:T(8,128)S(1)} collective-permute-done((f32[16,2048]{1,0:T(8,128)S(1)}, f32[16,2048]{1,0:T(8,128)S(1)}, u32[]{:S(2)}, u32[]{:S(2)}) %collective-permute-start.5) | collective-permute-done | bytes 131104 | tf_op jit(solution)/shard_map/ppermute | solution.py:18
  200.6 0.7 multiply_reduce_fusion
  201.3 9.3 %psum.7 = f32[2048]{0:T(1024)S(1)} all-reduce(f32[2048]{0:T(1024)S(1)} %get-tuple-element.2), channel_id=1, replica_groups=mesh['tok'=4,'ch'=8] {'tok'}, use_global_device_ids=true, to_apply=%region_1.2 | all-reduce | flops 2048 | bytes 16384 | tf_op jit(solution)/shard_map/psum | solution.py:478
  210.6 0.6 broadcast_multiply_fusion
  (31 shorter events, 0.5 us)
Async XLA Ops:
  2.9 1.5 collective-permute-start
  4.4 6.8 %collective-permute-start.1 = (f32[16,2048]{1,0:T(8,128)S(1)}, f32[16,2048]{1,0:T(8,128)S(1)}, u32[]{:S(2)}, u32[]{:S(2)}) collective-permute-start(f32[16,2048]{1,0:T(8,128)S(1)} %add_select_fusion.3), channel_id=1, source_target_pairs={{0,2},{1,3},{2,0},{3,1},{4,6},{5,7},{6,4},{7,5},{8,10},{9,11},{10,... | collective-permute-start | bytes 393224 | tf_op jit(solution)/shard_map/ppermute | solution.py:18
  11.3 8.8 %collective-permute-start.2 = (f32[16,2048]{1,0:T(8,128)S(1)}, f32[16,2048]{1,0:T(8,128)S(1)}, u32[]{:S(2)}, u32[]{:S(2)}) collective-permute-start(f32[16,2048]{1,0:T(8,128)S(1)} %add_select_fusion.2), channel_id=1, source_target_pairs={{0,4},{1,5},{2,6},{3,7},{4,0},{5,1},{6,2},{7,3},{8,12},{9,13},{10,... | collective-permute-start | bytes 393224 | tf_op jit(solution)/shard_map/ppermute | solution.py:18
  21.6 170.6 %copy-start.1 = (s32[2048]{0:T(1024)S(1)}, s32[2048]{0:T(1024)}, u32[]{:S(2)}) copy-start(s32[2048]{0:T(1024)} %param.8) | copy-start | bytes 24580
  21.6 179.0 %copy-start = (s32[16,2048]{1,0:T(8,128)S(1)}, s32[16,2048]{1,0:T(8,128)}, u32[]{:S(2)}) copy-start(s32[16,2048]{1,0:T(8,128)} %param.7) | copy-start | bytes 393220
  185.0 1.4 collective-permute-start.3
  186.5 5.6 %collective-permute-start.4 = (f32[16,2048]{1,0:T(8,128)S(1)}, f32[16,2048]{1,0:T(8,128)S(1)}, u32[]{:S(2)}, u32[]{:S(2)}) collective-permute-start(f32[16,2048]{1,0:T(8,128)S(1)} %add_select_fusion.1), channel_id=1, source_target_pairs={{0,2},{1,3},{2,0},{3,1},{4,6},{5,7},{6,4},{7,5},{8,10},{9,11},{10,... | collective-permute-start | bytes 393224 | tf_op jit(solution)/shard_map/ppermute | solution.py:18
  192.1 8.5 %collective-permute-start.5 = (f32[16,2048]{1,0:T(8,128)S(1)}, f32[16,2048]{1,0:T(8,128)S(1)}, u32[]{:S(2)}, u32[]{:S(2)}) collective-permute-start(f32[16,2048]{1,0:T(8,128)S(1)} %add_select_fusion), channel_id=1, source_target_pairs={{0,4},{1,5},{2,6},{3,7},{4,0},{5,1},{6,2},{7,3},{8,12},{9,13},{10,... | collective-permute-start | bytes 393224 | tf_op jit(solution)/shard_map/ppermute | solution.py:18

commit v2 on v1

--- a/solution.py
+++ b/solution.py
@@ -12,60 +12,48 @@
 VMEM_LIMIT = 63 * 1024 * 1024
 
 
-def partner_2(value, axis, stride):
-    mask = 2**stride
-    pairs = [(source, source ^ mask) for source in range(lax.axis_size(axis))]
-    return lax.ppermute(value, axis, pairs)
-
-
-def local_rotation(values):
-    rows, length = values.shape
-    lane = 128
-    index = jnp.arange(lane, dtype=jnp.int32)
-    parity = lax.population_count(index[:, None] & index[None, :]) & 1
-    inner = jnp.where(parity == 0, 1.0, -1.0).astype(jnp.float32)
-    values = jnp.dot(
-        values.reshape(rows * (length // lane), lane),
-        inner,
-        precision=lax.Precision.HIGHEST,
-        preferred_element_type=jnp.float32,
-    ).reshape(rows, length // lane, lane)
+LANE = 128
+SLOTS = 3
+HOP = 2
+NT = (((1,), (1,)), ((), ()))
+
+
+def butterfly(parts):
     span = 1
-    while span < length // lane:
-        pairs = values.reshape(rows, length // lane // (2 * span), 2, span, lane)
-        low, high = pairs[:, :, 0], pairs[:, :, 1]
-        values = jnp.stack([low + high, low - high], axis=2)
+    while span < len(parts):
+        for n in range(len(parts)):
+            if n & span == 0:
+                low, high = parts[n], parts[n + span]
+                parts[n], parts[n + span] = low + high, low - high
         span *= 2
-    return values.reshape(rows, length)
-
-
-def cross_pairs(values):
-    my_index = lax.axis_index("ch")
-    for bit_pos in range(lax.axis_size("ch").bit_length() - 1):
-        partner = partner_2(values, "ch", bit_pos)
-        upper_half = my_index >> bit_pos & 1 == 1
-        values = jnp.where(upper_half, partner - values, values + partner)
-    return values
-
-
-def cross_section(values):
-    return cross_pairs(values)
-
-
-SLOTS = 3
-NT = (((1,), (1,)), ((), ()))
-
-
-def layer_kernel(dims, x_in, gate_hbm, up_hbm, down_hbm, out_ref, *scratch):
-    shards, rows, zs, chunks, width = dims
+    return parts
+
+
+def rotate_local(values, inner, precision):
+    rows, lane = values.shape[0], inner.shape[0]
+    groups = values.shape[1] // lane
+    stacked = jnp.concatenate([values[:, g * lane : (g + 1) * lane] for g in range(groups)], axis=0)
+    turned = jnp.dot(stacked, inner, precision=precision, preferred_element_type=jnp.float32)
+    parts = butterfly([turned[g * rows : (g + 1) * rows] for g in range(groups)])
+    return jnp.concatenate(parts, axis=1)
+
+
+def layer_kernel(
+    dims, tokens_in, probe, signs, inner, gate_hbm, up_hbm, down_hbm, out_ref, diag_ref, *scratch
+):
+    shards, rows, ways, chunks, width, owners = dims
+    zs = ways // 2
     (
         x, gate_buf, up_buf, down_buf, sums, to_sib, from_sib, from_z, slope_up, active, hid,
         out_acc, o_send, o_recv, o_all, sums2, to_sib2, from_sib2, to_z2, from_z2, grads,
-        in_acc, k_send, k_recv,
+        k_send, k_recv, x_in, t_own, t_got, t_sum, t_res, f_own, f_got, f_sum, f_res,
+        diag_own, diag_got,
         gate_sem, up_sem, down_sem, x_ss, x_rs, os_ss, os_rs, og_ss, og_rs, k_ss, k_rs,
         a_ss, a_rs, b_ss, b_rs, d_ss, d_rs, s_ss, s_rs,
         a2_ss, a2_rs, b2_ss, b2_rs, d2_ss, d2_rs, s2_ss, s2_rs,
+        t1_ss, t1_rs, t2_ss, t2_rs, f1_ss, f1_rs, f2_ss, f2_rs, g_ss, g_rs,
     ) = scratch
+    in_acc = out_acc
     tok = lax.axis_index("tok")
     ch = lax.axis_index("ch")
     z, core = ch // 2, ch % 2
@@ -106,12 +94,64 @@
 
     for d in range(1, shards):
         greet(lax.rem(tok + d, shards), ch)
-    greet(tok, sib)
-    pl.when(z > 0)(lambda: greet(tok, ch - 2))
-    pl.when(z < last)(lambda: greet(tok, ch + 2))
-    inner = jnp.logical_and(z > 0, z < last)
-    pl.when(inner)(lambda: pl.semaphore_wait(barrier, shards + 2))
-    pl.when(jnp.logical_not(inner))(lambda: pl.semaphore_wait(barrier, shards + 1))
+    for d in range(1, ways):
+        greet(tok, lax.rem(ch + d, ways))
+    pl.semaphore_wait(barrier, shards + ways - 2)
+
+    def only(index, run):
+        if owners == ways:
+            run()
+        else:
+            pl.when(index < owners)(run)
+
+    def across(own, got, summed, res, ss1, rs1, ss2, rs2):
+        others = range(1, ways)
+        to = {d: lax.rem(ch + d, ways) for d in others}
+        of = {d: lax.rem(ch + ways - d, ways) for d in others}
+
+        def out1(d):
+            return remote(own.at[to[d]], got.at[ch], ss1.at[d], rs1.at[ch], tok, to[d])
+
+        def in1(d):
+            return remote(own.at[0], got.at[of[d]], ss1.at[d], rs1.at[of[d]], tok, of[d])
+
+        def out2(d):
+            return remote(summed.at[to[d]], res.at[ch], ss2.at[d], rs2.at[ch], tok, to[d])
+
+        def in2(d):
+            return remote(summed.at[0], res.at[of[d]], ss2.at[d], rs2.at[of[d]], tok, of[d])
+
+        for d in others:
+            only(to[d], lambda: out1(d).start())
+
+        def combine():
+            got[ch] = own[ch]
+            for d in others:
+                in1(d).wait_recv()
+            parts = butterfly([got[n].astype(f32) for n in range(ways)])
+            for n in range(ways):
+                summed[n] = parts[n].astype(summed.dtype)
+            for d in others:
+                out2(d).start()
+            res[ch] = summed[ch]
+
+        only(ch, combine)
+        for d in others:
+            only(of[d], lambda: in2(d).wait_recv())
+            only(to[d], lambda: out1(d).wait_send())
+        only(ch, lambda: [out2(d).wait_send() for d in others] and None)
+
+    root_scale = 1.0 / math.sqrt(D)
+    piece = tokens_in.shape[1] // owners
+    channel_signs = (2 * signs[...] - 1).astype(f32)
+    probe_signs = (2 * probe[...] - 1).astype(f32)
+    start = (probe_signs * channel_signs).astype(bf16)
+    for n in range(owners):
+        t_own[n] = start[:, n * piece : (n + 1) * piece]
+    across(t_own, t_got, t_sum, t_res, t1_ss, t1_rs, t2_ss, t2_rs)
+    start = jnp.concatenate([t_res[n] for n in range(owners)], axis=1)
+    x_in[:rows] = tokens_in[...]
+    x_in[rows:] = (rotate_local(start, inner[...], None) * root_scale).astype(bf16)
 
     def place(s):
         owner = s // per
@@ -145,7 +185,7 @@
     def when(*conditions):
         return pl.when(functools.reduce(jnp.logical_and, conditions))
 
-    def line(i, chunk_at, part, add_sib, a_copy, recv, b_copy, finish, block, d_copy, s_copy):
+    def line(i, hop, chunk_at, part, add_sib, a_copy, recv, b_copy, finish, d_copy, s_copy):
         n1 = i - 1
 
         @pl.when(in_range(n1))
@@ -154,7 +194,7 @@
             add_sib(chunk_at(n1))
 
         for e, far, near, toward, away in ends():
-            n2 = i - 1 - far
+            n2 = i - 1 - hop * far
 
             @pl.when(in_range(n2))
             def _():
@@ -176,7 +216,7 @@
                     d_copy(e, f, away).start()
                     s_copy(e, f).start()
 
-            n3 = i - 1 - last - near
+            n3 = i - 1 - hop * last - near
 
             @when(in_range(n3), near > 0)
             def _():
@@ -200,7 +240,7 @@
 
         lax.fori_loop(0, chunks, body, 0)
 
-    lag = 2 + 2 * last
+    lag, lag2 = 2 + (1 + HOP) * last, 2 + 2 * last
 
     def block_of(e):
         return pl.ds(pl.multiple_of((e * 2 + core) * quarter, quarter), quarter)
@@ -276,7 +316,7 @@
                     copy.start()
 
         line(
-            i, lambda n: n, lambda e, f: None, add_sib, a_copy, recv, b_copy, finish, None,
+            i, HOP, lambda n: n, lambda e, f: None, add_sib, a_copy, recv, b_copy, finish,
             d_copy, s_copy,
         )
         n4 = i - lag
@@ -371,9 +411,9 @@
             a2_copy(f).start()
 
         line(
-            i, chunk_at, part2, add_sib2, a2_copy, recv2, b2_copy, finish2, None, d2_copy, s2_copy
-        )
-        n4 = i - lag
+            i, 1, chunk_at, part2, add_sib2, a2_copy, recv2, b2_copy, finish2, d2_copy, s2_copy
+        )
+        n4 = i - lag2
 
         @pl.when(n4 >= 0)
         def _():
@@ -399,19 +439,39 @@
 
         return carry
 
-    lax.fori_loop(0, chunks + lag, backward, 0)
+    lax.fori_loop(0, chunks + lag2, backward, 0)
     drain(a2_copy, b2_copy, d2_copy, s2_copy)
-    out_ref[...] = scatter(in_acc, k_send, k_recv, k_ss, k_rs)
-
-
-def layer(local, gate_weight, up_weight, down_weight):
+    back_tokens = scatter(in_acc, k_send, k_recv, k_ss, k_rs)
+    turned = rotate_local(back_tokens, inner[...].astype(f32), lax.Precision.HIGHEST)
+    for n in range(owners):
+        f_own[n] = turned[:, n * piece : (n + 1) * piece]
+    across(f_own, f_got, f_sum, f_res, f1_ss, f1_rs, f2_ss, f2_rs)
+    turned = jnp.concatenate([f_res[n] for n in range(owners)], axis=1)
+    product = turned * root_scale * channel_signs
+    out_ref[...] = product
+    diag_own[...] = jnp.sum(probe_signs * product, axis=0, keepdims=True)
+    copies = peers(
+        lambda d, p: remote(diag_own, diag_got.at[d - 1], g_ss.at[d - 1], g_rs.at[d - 1], p, ch)
+    )
+    for copy in copies:
+        copy.start()
+    diagonal = diag_own[...]
+    for d, copy in enumerate(copies):
+        copy.wait()
+        diagonal = diagonal + diag_got[d]
+    diag_ref[...] = diagonal / (shards * rows)
+
+
+def layer(tokens, probe, signs, inner, gate_weight, up_weight, down_weight):
     shards, ways = lax.axis_size("tok"), lax.axis_size("ch")
-    rows, depth = local.shape[0] // 2, local.shape[1]
+    rows, depth = tokens.shape
     hidden = gate_weight.shape[1]
     width = max(w for w in range(128, 513, 128) if hidden % w == 0)
     chunks = hidden // width
     total, quarter = shards * rows, shards * rows // 4
-    dims = (shards, rows, ways // 2, chunks, width)
+    owners = min(ways, depth // LANE)
+    piece = depth // owners
+    dims = (shards, rows, ways, chunks, width, owners)
     f32, bf16, vmem = jnp.float32, jnp.bfloat16, pltpu.VMEM
     dma = pltpu.SemaphoreType.DMA
     scratch = [
@@ -436,21 +496,29 @@
         vmem((chunks, 2, quarter, width), bf16),
         vmem((chunks, 2, quarter, width), bf16),
         vmem((chunks, 4, 2, quarter, width), bf16),
-        vmem((total, depth), f32),
         vmem((total, depth), bf16),
         vmem((shards - 1, rows, depth), bf16),
+        vmem((2 * rows, depth), bf16),
+        *[vmem((n, rows, piece), bf16) for n in (owners, ways, ways, owners)],
+        *[vmem((n, rows, piece), f32) for n in (owners, ways, ways, owners)],
+        vmem((1, depth), f32),
+        vmem((shards - 1, 1, depth), f32),
         dma((SLOTS,)), dma((SLOTS,)), dma((chunks,)),
         *[dma((shards - 1,)) for _ in range(8)],
     ]
     for _ in range(2):
         scratch += [dma((chunks,)), dma((chunks,))]
         scratch += [dma((2, chunks)) for _ in range(6)]
+    scratch += [dma((ways,)) for _ in range(8)] + [dma((shards - 1,)) for _ in range(2)]
     flops = 2 * total * depth * hidden * 8
     return pl.pallas_call(
         functools.partial(layer_kernel, dims),
-        out_shape=jax.ShapeDtypeStruct((rows, depth), f32),
-        in_specs=[pl.BlockSpec(memory_space=vmem)] + [pl.BlockSpec(memory_space=pl.ANY)] * 3,
-        out_specs=pl.BlockSpec(memory_space=vmem),
+        out_shape=(
+            jax.ShapeDtypeStruct((rows, depth), f32),
+            jax.ShapeDtypeStruct((1, depth), f32),
+        ),
+        in_specs=[pl.BlockSpec(memory_space=vmem)] * 4 + [pl.BlockSpec(memory_space=pl.ANY)] * 3,
+        out_specs=(pl.BlockSpec(memory_space=vmem), pl.BlockSpec(memory_space=vmem)),
         scratch_shapes=scratch,
         compiler_params=pltpu.CompilerParams(
             collective_id=0, has_side_effects=True, vmem_limit_bytes=VMEM_LIMIT
@@ -458,25 +526,17 @@
         cost_estimate=pl.CostEstimate(
             flops=flops, bytes_accessed=10 * depth * hidden, transcendentals=0
         ),
-    )(local, gate_weight, up_weight, down_weight)
+    )(tokens, probe, signs, inner, gate_weight, up_weight, down_weight)
 
 
 def on_device(tokens, probe, signs, gate_weight, up_weight, down_weight):
-    tok_rows, channels = tokens.shape
-    total_rows = tok_rows * lax.axis_size("tok")
-    root_scale = 1.0 / math.sqrt(D)
-    probe_signs = (2 * probe - 1).astype(jnp.float32)
-    channel_signs = (2 * signs - 1).astype(jnp.float32)
-    start_local = local_rotation(probe_signs * channel_signs[None, :])
-    tangent = (cross_section(start_local) * root_scale).astype(jnp.bfloat16)
-    back_tokens = layer(
-        jnp.concatenate([tokens, tangent], axis=0), gate_weight, up_weight, down_weight
+    index = jnp.arange(LANE, dtype=jnp.int32)
+    parity = lax.population_count(index[:, None] & index[None, :]) & 1
+    inner = jnp.where(parity == 0, 1.0, -1.0).astype(jnp.bfloat16)
+    rotated_product, diagonal_estimate = layer(
+        tokens, probe, signs[None, :], inner, gate_weight, up_weight, down_weight
     )
-    local_back = local_rotation(back_tokens)
-    rotated_product = cross_section(local_back) * root_scale * channel_signs[None, :]
-    token_terms = jnp.sum(probe_signs * rotated_product, axis=0)
-    diagonal_estimate = lax.psum(token_terms, "tok") / total_rows
-    return (rotated_product, diagonal_estimate)
+    return (rotated_product, diagonal_estimate[0])
 
 
 def solution(mesh):

time: 212 us -> 179 us (0.84)
  waiting for transfers between devices: 26 us -> 0 us
  Pallas kernels: 162 us -> 174 us
  blocking collectives: 9.32 us -> 0 us
  starting transfers between devices: 6.59 us -> 0 us
  other arithmetic: 4.76 us -> 0.63 us
    ppermute x6 -> x0, waiting for transfers between devices: 26 us -> none  [partner_2(): return lax.ppermute(value, axis, pairs)]
    pallas_call x1, Pallas kernels: 162 us -> 174 us  [layer(): pl.pallas_call(functools.partial(layer_kernel, dims), out_shape=(jax.Shap...]
    psum x1 -> x0, blocking collectives: 9.32 us -> none  [on_device(): diagonal_estimate = lax.psum(token_terms, 'tok') / total_rows]
    ppermute x6 -> x0, starting transfers between devices: 6.59 us -> none  [partner_2(): return lax.ppermute(value, axis, pairs)]
    unnamed x6 -> x2, local copies, waits for them, and re-layouts: 0.04 us -> 2.86 us
  transfers between devices with their start and end apart: 6 -> 0, of which waited for: 6 -> 0; matrix products, arithmetic and copies ran while one was open for 0% -> 0% of each run, Pallas kernels for 0% -> 0%
where the time goes in v2:
time: 179 us; the launch traced here: 178 us
  Pallas kernels  174 us (97%)
  local copies, waits for them, and re-layouts  2.86 us (2%)
    pallas_call x1, Pallas kernels, layer(): pl.pallas_call(functools.partial(layer_kernel, dims), out_shape=(jax.Shap...  174 us

profile of v2, /device:TPU:0, one launch (start us, length us, event | category | flops | bytes accessed | tf_op | source)
XLA Modules:
  0.0 178.5 jit_solution(18329365697933377410)
XLA Ops:
  0.6 0.6 select_convert_fusion.inner
  1.3 174.3 %shard_map.77 = (f32[16,2048]{1,0:T(8,128)}, f32[1,2048]{1,0:T(1,128)}) custom-call(bf16[16,2048]{1,0:T(8,128)(2,1)} %tokens_in.1, s32[16,2048]{1,0:T(8,128)} %probe.1, s32[1,2048]{1,0:T(1,128)} %bitcast.2, bf16[128,128]{1,0:T(8,128)(2,1)} %select_convert_fusion.inner, bf16[2048,6656]{1,0:T(8,128)(2,1)} %gate_hbm.1, bf16[2048,6656]{1,0:T(8,128)(2,1)} %up_hbm.1, ...), custom_call_target="tpu_custom_call" | custom-call | flops 13958643712 | bytes 136314880 | tf_op jit(solution)/shard_map/pallas_call | solution.py:514
  175.6 1.6 copy.10
  177.2 1.3 copy.11

commit v3 on v2

--- a/solution.py
+++ b/solution.py
@@ -16,6 +16,23 @@
 SLOTS = 3
 HOP = 2
 NT = (((1,), (1,)), ((), ()))
+
+
+class Pair:
+    def __init__(self, *copies):
+        self.copies = copies
+
+    def start(self):
+        for copy in self.copies:
+            copy.start()
+
+    def wait_recv(self):
+        for copy in self.copies:
+            copy.wait_recv()
+
+    def wait_send(self):
+        for copy in self.copies:
+            copy.wait_send()
 
 
 def butterfly(parts):
@@ -44,16 +61,15 @@
     shards, rows, ways, chunks, width, owners = dims
     zs = ways // 2
     (
-        x, gate_buf, up_buf, down_buf, sums, to_sib, from_sib, from_z, slope_up, active, hid,
-        out_acc, o_send, o_recv, o_all, sums2, to_sib2, from_sib2, to_z2, from_z2, grads,
-        k_send, k_recv, x_in, t_own, t_got, t_sum, t_res, f_own, f_got, f_sum, f_res,
+        x, gate_buf, up_buf, down_buf, sums, to_sib, from_sib, from_z, to_zt, from_zt, slope_up, active, hid,
+        out_acc, o_send, o_recv, o_all, from_z2, grads,
+        in_acc, k_recv, x_in, t_own, t_got, t_sum, t_res, f_own, f_got, f_sum, f_res,
         diag_own, diag_got,
         gate_sem, up_sem, down_sem, x_ss, x_rs, os_ss, os_rs, og_ss, og_rs, k_ss, k_rs,
         a_ss, a_rs, b_ss, b_rs, d_ss, d_rs, s_ss, s_rs,
         a2_ss, a2_rs, b2_ss, b2_rs, d2_ss, d2_rs, s2_ss, s2_rs,
-        t1_ss, t1_rs, t2_ss, t2_rs, f1_ss, f1_rs, f2_ss, f2_rs, g_ss, g_rs,
+        t1_ss, t1_rs, t2_ss, t2_rs, f1_ss, f1_rs, f2_ss, f2_rs, g_ss, g_rs, t_ss, t_rs,
     ) = scratch
-    in_acc = out_acc
     tok = lax.axis_index("tok")
     ch = lax.axis_index("ch")
     z, core = ch // 2, ch % 2
@@ -251,8 +267,9 @@
         return remote(to_sib.at[f], from_sib.at[f], a_ss.at[f], a_rs.at[f], tok, sib)
 
     def b_copy(e, f, c):
-        return remote(
-            sums.at[f, e], from_z.at[f, e], b_ss.at[e, f], b_rs.at[e, f], tok, c
+        return Pair(
+            remote(sums.at[f, e, :, 0], from_z.at[f, e], b_ss.at[e, f], b_rs.at[e, f], tok, c),
+            remote(to_zt.at[f, e], from_zt.at[f, e], t_ss.at[e, f], t_rs.at[e, f], tok, c),
         )
 
     def d_copy(e, f, c):
@@ -272,15 +289,18 @@
         sums[f] += from_sib[f]
 
     def recv(e, f):
-        sums[f, e] += from_z[f, e]
+        sums[f, e, :, 0] += from_z[f, e]
+        sums[f, e, :, 1] += from_zt[f, e].astype(f32)
+
+    def part1(e, f):
+        to_zt[f, e] = sums[f, e, :, 1].astype(bf16)
 
     def finish(e, f):
         for p in range(per):
-            base = p * 2 * rows
-            gate_pre = sums[f, e, base : base + rows, :width]
-            up_pre = sums[f, e, base : base + rows, width:]
-            gate_tan = sums[f, e, base + rows : base + 2 * rows, :width]
-            up_tan = sums[f, e, base + rows : base + 2 * rows, width:]
+            gate_pre = sums[f, e, p, 0, :, :width]
+            up_pre = sums[f, e, p, 0, :, width:]
+            gate_tan = sums[f, e, p, 1, :, :width]
+            up_tan = sums[f, e, p, 1, :, width:]
             sig = jax.nn.sigmoid(gate_pre)
             act = gate_pre * sig
             slope = sig * (1.0 + gate_pre * (1.0 - sig))
@@ -304,10 +324,10 @@
             for n, buf in enumerate((gate_buf, up_buf)):
                 part = jnp.dot(x[...], buf[slot], preferred_element_type=f32)
                 cols = slice(n * width, (n + 1) * width)
+                part = part.reshape(4, per, 2, rows, width)
                 for e in range(2):
-                    sums[i, e, :, cols] = part[e * 2 * quarter : (e + 1) * 2 * quarter]
-                to_sib[i, 0, :, cols] = part[4 * quarter : 6 * quarter]
-                to_sib[i, 1, :, cols] = part[6 * quarter :]
+                    sums[i, e, :, :, :, cols] = part[e]
+                    to_sib[i, e, :, :, :, cols] = part[2 + e]
             a_copy(i).start()
 
             @pl.when(i + SLOTS < chunks)
@@ -316,7 +336,7 @@
                     copy.start()
 
         line(
-            i, HOP, lambda n: n, lambda e, f: None, add_sib, a_copy, recv, b_copy, finish,
+            i, HOP, lambda n: n, part1, add_sib, a_copy, recv, b_copy, finish,
             d_copy, s_copy,
         )
         n4 = i - lag
@@ -362,11 +382,13 @@
         copy.wait()
 
     def a2_copy(f):
-        return remote(to_sib2.at[f], from_sib2.at[f], a2_ss.at[f], a2_rs.at[f], tok, sib)
+        at = (f, slice(None), slice(None), 0, slice(None), pl.ds(0, width))
+        return remote(to_sib.at[at], from_sib.at[at], a2_ss.at[f], a2_rs.at[f], tok, sib)
 
     def b2_copy(e, f, c):
+        src = sums.at[f, e, :, 0, :, pl.ds(0, width)]
         return remote(
-            to_z2.at[f, e], from_z2.at[f, e], b2_ss.at[e, f], b2_rs.at[e, f], tok, c
+            src, from_z2.at[f, e], b2_ss.at[e, f], b2_rs.at[e, f], tok, c
         )
 
     def d2_copy(e, f, c):
@@ -382,16 +404,13 @@
         return remote(ref, ref, s2_ss.at[e, f], s2_rs.at[e, f], tok, sib)
 
     def add_sib2(f):
-        sums2[f] += from_sib2[f]
+        sums[f, :, :, 0, :, :width] += from_sib[f, :, :, 0, :, :width]
 
     def recv2(e, f):
-        sums2[f, e] += from_z2[f, e].astype(f32)
-
-    def part2(e, f):
-        to_z2[f, e] = sums2[f, e].astype(bf16)
+        sums[f, e, :, 0, :, :width] += from_z2[f, e]
 
     def finish2(e, f):
-        back = sums2[f, e]
+        back = sums[f, e, :, 0, :, :width].reshape(quarter, width)
         grads[f, e * 2 + core, 0] = (back * slope_up[f]).astype(bf16)
         grads[f, e * 2 + core, 1] = (back * active[f]).astype(bf16)
 
@@ -404,14 +423,15 @@
         @pl.when(i < chunks)
         def _():
             f = chunk_at(i)
-            part = lax.dot_general(o_all[...], down_buf[f], NT, preferred_element_type=f32)
+            part = lax.dot_general(down_buf[f], o_all[...], NT, preferred_element_type=f32).T
+            part = part.reshape(4, per, rows, width)
             for e in range(2):
-                sums2[f, e] = part[e * quarter : (e + 1) * quarter]
-                to_sib2[f, e] = part[(2 + e) * quarter : (3 + e) * quarter]
+                sums[f, e, :, 0, :, :width] = part[e]
+                to_sib[f, e, :, 0, :, :width] = part[2 + e]
             a2_copy(f).start()
 
         line(
-            i, 1, chunk_at, part2, add_sib2, a2_copy, recv2, b2_copy, finish2, d2_copy, s2_copy
+            i, 1, chunk_at, lambda e, f: None, add_sib2, a2_copy, recv2, b2_copy, finish2, d2_copy, s2_copy
         )
         n4 = i - lag2
 
@@ -430,7 +450,7 @@
             both = grads[f]
             for n, buf in enumerate((gate_buf, up_buf)):
                 piece = both[:, n].reshape(4 * quarter, width)
-                in_acc[...] += lax.dot_general(piece, buf[slot], NT, preferred_element_type=f32)
+                in_acc[...] += lax.dot_general(buf[slot], piece, NT, preferred_element_type=f32)
 
             @pl.when(f >= SLOTS)
             def _():
@@ -441,7 +461,8 @@
 
     lax.fori_loop(0, chunks + lag2, backward, 0)
     drain(a2_copy, b2_copy, d2_copy, s2_copy)
-    back_tokens = scatter(in_acc, k_send, k_recv, k_ss, k_rs)
+    out_acc[...] = in_acc[...].T
+    back_tokens = scatter(out_acc, o_send, k_recv, k_ss, k_rs)
     turned = rotate_local(back_tokens, inner[...].astype(f32), lax.Precision.HIGHEST)
     for n in range(owners):
         f_own[n] = turned[:, n * piece : (n + 1) * piece]
@@ -471,6 +492,7 @@
     total, quarter = shards * rows, shards * rows // 4
     owners = min(ways, depth // LANE)
     piece = depth // owners
+    per = shards // 4
     dims = (shards, rows, ways, chunks, width, owners)
     f32, bf16, vmem = jnp.float32, jnp.bfloat16, pltpu.VMEM
     dma = pltpu.SemaphoreType.DMA
@@ -479,10 +501,8 @@
         vmem((SLOTS, depth, width), bf16),
         vmem((SLOTS, depth, width), bf16),
         vmem((chunks, width, depth), bf16),
-        vmem((chunks, 2, 2 * quarter, 2 * width), f32),
-        vmem((chunks, 2, 2 * quarter, 2 * width), f32),
-        vmem((chunks, 2, 2 * quarter, 2 * width), f32),
-        vmem((chunks, 2, 2 * quarter, 2 * width), f32),
+        *[vmem((chunks, 2, per, 2, rows, 2 * width), f32) for _ in range(3)],
+        *[vmem((chunks, 2, per, rows, 2 * width), kind) for kind in (f32, bf16, bf16)],
         vmem((chunks, quarter, width), f32),
         vmem((chunks, quarter, width), f32),
         vmem((chunks, total, width), bf16),
@@ -490,13 +510,9 @@
         vmem((total, depth), bf16),
         vmem((shards - 1, rows, depth), bf16),
         vmem((total, depth), bf16),
-        vmem((chunks, 2, quarter, width), f32),
-        vmem((chunks, 2, quarter, width), f32),
-        vmem((chunks, 2, quarter, width), f32),
-        vmem((chunks, 2, quarter, width), bf16),
-        vmem((chunks, 2, quarter, width), bf16),
+        vmem((chunks, 2, per, rows, width), f32),
         vmem((chunks, 4, 2, quarter, width), bf16),
-        vmem((total, depth), bf16),
+        vmem((depth, total), f32),
         vmem((shards - 1, rows, depth), bf16),
         vmem((2 * rows, depth), bf16),
         *[vmem((n, rows, piece), bf16) for n in (owners, ways, ways, owners)],
@@ -510,6 +526,7 @@
         scratch += [dma((chunks,)), dma((chunks,))]
         scratch += [dma((2, chunks)) for _ in range(6)]
     scratch += [dma((ways,)) for _ in range(8)] + [dma((shards - 1,)) for _ in range(2)]
+    scratch += [dma((2, chunks)), dma((2, chunks))]
     flops = 2 * total * depth * hidden * 8
     return pl.pallas_call(
         functools.partial(layer_kernel, dims),

time: 179 us -> 171 us (0.955)
  Pallas kernels: 174 us -> 167 us
    pallas_call x1, Pallas kernels: 174 us -> 167 us  [layer(): pl.pallas_call(functools.partial(layer_kernel, dims), out_shape=(jax.Shap...]
where the time goes in v3:
time: 171 us
  Pallas kernels  167 us (98%)
  local copies, waits for them, and re-layouts  2.86 us (2%)
    pallas_call x1, Pallas kernels, layer(): pl.pallas_call(functools.partial(layer_kernel, dims), out_shape=(jax.Shap...  167 us

profile of v3, /device:TPU:0, one launch (start us, length us, event | category | flops | bytes accessed | tf_op | source)
XLA Modules:
  0.0 171.1 jit_solution(17526577284097784119)
XLA Ops:
  0.6 0.6 select_convert_fusion.inner
  1.3 167.0 %shard_map.77 = (f32[16,2048]{1,0:T(8,128)}, f32[1,2048]{1,0:T(1,128)}) custom-call(bf16[16,2048]{1,0:T(8,128)(2,1)} %tokens_in.1, s32[16,2048]{1,0:T(8,128)} %probe.1, s32[1,2048]{1,0:T(1,128)} %bitcast.2, bf16[128,128]{1,0:T(8,128)(2,1)} %select_convert_fusion.inner, bf16[2048,6656]{1,0:T(8,128)(2,1)} %gate_hbm.1, bf16[2048,6656]{1,0:T(8,128)(2,1)} %up_hbm.1, ...), custom_call_target="tpu_custom_call" | custom-call | flops 13958643712 | bytes 136314880 | tf_op jit(solution)/shard_map/pallas_call | solution.py:531
  168.2 1.6 copy.10
  169.8 1.3 copy.11
